TPU v7x, 32 devices: a whole 2x2x4 slice. The times are simulated.
32 devices in a mesh: groups: 2 (over y), query: 2 (over x), car: 4 (over z), replica: 2 (over core).
Axes of the slice: x: 2, y: 2, z: 4, core: 2. Of those that a mesh axis runs over, the one named last changes fastest.
Arguments:
- query_heads: bfloat16 [16384, 768], P(('groups', 'query', 'car', 'replica')), parts along dimension 0, may hold values from -140 to 140
- d_out: bfloat16 [16384, 768], P(('groups', 'query', 'car', 'replica')), parts along dimension 0, may hold values from -0.375 to 0.375
- anchor_kv: bfloat16 [8, 8, 1536], P(('groups', 'car'), 'query'), parts along dimension 0, may hold values from -8 to 8
- point_counts: int32 [32, 4], P(('groups', 'query', 'car', 'replica')), parts along dimension 0, may hold values from 1 to 256, 512 in all within a row
- slot_car: int32 [8], P('groups'), parts along dimension 0, may hold values from 0 to 3, each once
- out_weight: bfloat16 [768, 768], replicated, may hold values from -1.75 to 1.75
Outputs:
- grad_queries: bfloat16 [16384, 768], P(('groups', 'query', 'car', 'replica')), parts along dimension 0
- grad_kv: float32 [8, 8, 1536], P(('groups', 'car'), 'query'), parts along dimension 0
- grad_out_weight: float32 [1536, 768], P('groups'), parts along dimension 0
There are 2 independent parts, one for each index of `groups`. A program takes and returns all parts, laid end to end along the dimension named above; an argument that names none is the same for every part. Nothing has to cross between parts.
Inputs may be any that keep to these rules, and one draw needn't show every extreme that they name: `point_counts`: in every shard some car has exactly 256 points. `slot_car`: each car stands in exactly one slot.
All inputs are finite; a program needn't handle non-finite values.
Results may differ from a plain program's by a relative error of at most 0.013.
Values may be sent and summed in bfloat16 or wider, within the bound.
A program may use at most 64 MiB of HBM per device.

v0:
```python
import math

import jax
import jax.numpy as jnp
from jax import lax
from jax.sharding import PartitionSpec as P

D = 768
HEADS = 12
HEAD_DIM = 64


def head_view(values):
    return values.reshape(values.shape[0], HEADS, HEAD_DIM)


def car_lookup(start, count, anchors_each, owners, slot_car):
    rows = start + jnp.arange(count, dtype=jnp.int32)
    slots = rows // anchors_each % owners
    table = slots[:, None] == jnp.arange(slot_car.shape[0], dtype=jnp.int32)[None, :]
    return jnp.sum(jnp.where(table, slot_car[None, :], 0), axis=1)


def body(query_heads, d_out, anchor_kv, point_counts, slot_car, out_weight):
    scale = HEAD_DIM ** (-0.5)
    owners = lax.axis_size("car")
    anchors_each = anchor_kv.shape[1]
    rows_here = query_heads.shape[0]
    ends = jnp.cumsum(point_counts[0])
    local = jnp.arange(rows_here, dtype=jnp.int32)
    point_car = jnp.sum((local[:, None] >= ends[None, :]).astype(jnp.int32), axis=1)
    panel = anchor_kv[0]
    queries = head_view(query_heads)

    def allowed_for(start, count):
        cars = car_lookup(start, count, anchors_each, owners, slot_car)
        return (point_car[:, None] == cars[None, :])[:, None, :]

    def forward_step(carry, piece, start):
        best, total, accum = carry
        count = piece.shape[0]
        keys = head_view(piece[:, :D])
        values = head_view(piece[:, D:])
        allowed = allowed_for(start, count)
        scores = (
            jnp.einsum("qhe,khe->qhk", queries, keys, preferred_element_type=jnp.float32) * scale
        )
        peak = jnp.max(jnp.where(allowed, scores, -1e30), axis=2)
        new_best = jnp.maximum(best, peak)
        weights = jnp.where(allowed, jnp.exp(scores - new_best[:, :, None]), 0.0)
        fade = jnp.exp(best - new_best)
        total = total * fade + jnp.sum(weights, axis=2)
        accum = accum * fade[:, :, None] + jnp.einsum(
            "qhk,khe->qhe", weights.astype(jnp.bfloat16), values, preferred_element_type=jnp.float32
        )
        return (new_best, total, accum)

    init = (
        jnp.full((rows_here, HEADS), -1e30, jnp.float32),
        jnp.zeros((rows_here, HEADS), jnp.float32),
        jnp.zeros((rows_here, HEADS, HEAD_DIM), jnp.float32),
    )
    kv_all = lax.all_gather(panel, ("query", "car"), axis=0, tiled=True)
    key_rows = kv_all.shape[0]
    block = math.gcd(key_rows, 128)
    blocks = kv_all.reshape(key_rows // block, block, 2 * D)

    def scan_forward(carry, inputs):
        piece, number = inputs
        return (forward_step(carry, piece, number * block), None)

    (best, total, accum), _ = lax.scan(
        scan_forward, init, (blocks, jnp.arange(key_rows // block, dtype=jnp.int32))
    )
    numbers = jnp.arange(key_rows // block, dtype=jnp.int32)
    attended = (accum / total[:, :, None]).reshape(rows_here, D).astype(jnp.bfloat16)
    d_att = lax.dot_general(
        d_out, out_weight, (((1,), (1,)), ((), ())), preferred_element_type=jnp.float32
    ).astype(jnp.bfloat16)
    weight_term = lax.dot_general(
        attended, d_out, (((0,), (0,)), ((), ())), preferred_element_type=jnp.float32
    )
    weight_grad = lax.psum(weight_term, ("query", "car", "replica"))
    d_heads = head_view(d_att)
    delta = jnp.sum(d_heads.astype(jnp.float32) * head_view(attended).astype(jnp.float32), axis=2)

    def backward_step(d_query, inputs):
        piece, number = inputs
        keys = head_view(piece[:, :D])
        values = head_view(piece[:, D:])
        allowed = allowed_for(number * block, block)
        scores = (
            jnp.einsum("qhe,khe->qhk", queries, keys, preferred_element_type=jnp.float32) * scale
        )
        prob = jnp.where(allowed, jnp.exp(scores - best[:, :, None]), 0.0) / total[:, :, None]
        d_prob = jnp.einsum("qhe,khe->qhk", d_heads, values, preferred_element_type=jnp.float32)
        d_score = (prob * (d_prob - delta[:, :, None])).astype(jnp.bfloat16)
        d_query = d_query + jnp.einsum(
            "qhk,khe->qhe", d_score, keys, preferred_element_type=jnp.float32
        )
        d_key = (
            jnp.einsum("qhk,qhe->khe", d_score, queries, preferred_element_type=jnp.float32) * scale
        )
        d_value = jnp.einsum(
            "qhk,qhe->khe", prob.astype(jnp.bfloat16), d_heads, preferred_element_type=jnp.float32
        )
        return (
            d_query,
            jnp.concatenate([d_key.reshape(block, D), d_value.reshape(block, D)], axis=1),
        )

    d_query, stacked = lax.scan(
        backward_step, jnp.zeros((rows_here, HEADS, HEAD_DIM), jnp.float32), (blocks, numbers)
    )
    kv_term = stacked.reshape(key_rows, 2 * D)
    kv_part = lax.psum_scatter(kv_term, ("query", "car"), scatter_dimension=0, tiled=True)
    kv_mine = lax.psum(kv_part, "replica")
    grad_queries = (d_query * scale).reshape(rows_here, D).astype(jnp.bfloat16)
    return (grad_queries, kv_mine.reshape(1, anchors_each, 2 * D), weight_grad)


def solution(mesh):
    in_specs = (
        P(("groups", "query", "car", "replica"), None),
        P(("groups", "query", "car", "replica"), None),
        P(("groups", "car"), "query", None),
        P(("groups", "query", "car", "replica"), None),
        P("groups"),
        P(),
    )
    out_specs = (
        P(("groups", "query", "car", "replica"), None),
        P(("groups", "car"), "query", None),
        P("groups", None),
    )
    return jax.shard_map(body, mesh=mesh, in_specs=in_specs, out_specs=out_specs, check_vma=False)
```

profile of v0, /device:TPU:1, one launch (start us, length us, event | category | flops | bytes accessed | tf_op | source)
XLA Modules:
  0.0 236.5 jit_solution(1861843765459569535)
XLA Ops:
  7.2 0.9 reduce-window.8
  8.2 0.1 convert_reduce_fusion
  8.2 0.7 copy.44
  9.0 26.1 %all-gather = bf16[1,32,1536]{2,0,1:T(2,128)(2,1)S(1)} all-gather(bf16[1,4,1536]{2,0,1:T(2,128)(2,1)S(1)} %copy.44), channel_id=2, replica_groups=mesh['groups'=2,'query'=2,'car'=4,'replica'=2] {'query','car'}, dimensions={1}, use_global_device_ids=true | all-gather | bytes 110592 | tf_op jit(solution)/shard_map/all_gather | solution.py:63
  35.1 0.1 reshape.133
  35.2 1.4 copy.45
  36.7 0.1 select_reduce_fusion.1
  36.8 0.1 broadcast_compare_fusion
  36.8 0.3 select_reduce_fusion
  37.1 0.2 fusion.9
  37.4 0.4 copy-done.2
  37.8 1.7 convolution_convert_fusion
  39.5 2.3 copy.47
  41.8 0.1 reshape.136
  42.0 1.5 convolution_bitcast_fusion.1
  43.5 1.5 multiply_reduce_fusion
  45.0 1.3 fusion.5
  46.2 0.3 fusion.6
  46.6 0.1 copy.51
  46.7 0.1 reshape.137
  46.8 0.1 copy.52
  46.9 0.1 reshape.138
  47.0 0.7 pad_maximum_fusion
  47.8 3.3 %fusion.25 = f32[768,768]{1,0:T(8,128)} fusion(bf16[512,768]{0,1:T(8,128)(2,1)} %bitcast.50, bf16[512,768]{1,0:T(8,128)(2,1)S(1)} %copy-done.3), kind=kOutput, calls=%fused_computation.50 | convolution fusion | flops 603979776 | bytes 3932160 | tf_op jit(solution)/shard_map/dot_general | solution.py:80
  51.2 0.4 multiply_convert_fusion
  51.6 1.2 copy.53
  52.8 0.6 dynamic-slice.1
  54.0 69.1 %all-reduce.6.cloned.1.call-done = f32[32,1536]{1,0:T(8,128)} async-done(((f32[32,1536]{1,0:T(8,128)}), f32[32,1536]{1,0:T(8,128)}) %all-reduce.6.cloned.1.call-update) | async-done | bytes 196624
  123.1 0.8 dynamic-slice_bitcast_fusion
  123.9 6.4 %psum.14 = f32[1,4,1536]{2,1,0:T(4,128)} all-reduce(f32[1,4,1536]{2,1,0:T(4,128)S(1)} %dynamic-slice_bitcast_fusion), channel_id=1, replica_groups=mesh['groups'=2,'query'=2,'car'=4,'replica'=2] {'replica'}, use_global_device_ids=true, to_apply=%region_7.8 | all-reduce | flops 6144 | bytes 49152 | tf_op jit(solution)/shard_map/psum | solution.py:117
  130.3 96.1 %all-reduce.4.cloned.1.call-done = f32[768,768]{1,0:T(8,128)} async-done(((f32[768,768]{1,0:T(8,128)}), f32[768,768]{1,0:T(8,128)}) %all-reduce.4.cloned.1.call-update) | async-done | bytes 2359312 | tf_op jit(solution)/shard_map/psum | solution.py:83
  226.4 3.2 %copy.71 = f32[768,768]{1,0:T(8,128)} copy(f32[768,768]{1,0:T(8,128)} %all-reduce.4.cloned.1.call-done) | data formatting | bytes 4718592
  (22 shorter events, 0.2 us)
Async XLA Ops:
  7.2 30.2 %copy-start = (bf16[768,768]{1,0:T(8,128)(2,1)S(1)}, bf16[768,768]{1,0:T(8,128)(2,1)}, u32[]{:S(2)}) copy-start(bf16[768,768]{1,0:T(8,128)(2,1)} %param.11) | copy-start | bytes 3538948
  7.2 29.5 %copy-start.5 = (s32[4]{0:T(128)S(1)}, s32[4]{0:T(128)}, u32[]{:S(2)}) copy-start(s32[4]{0:T(128)} %param.10) | copy-start | bytes 52
  7.2 115.9 %all-reduce.6.cloned.1.call-start = ((), (), s32[]{:S(2)}) async-start(), calls=%async_computation.1 | async-start | bytes 393216
  36.7 1.1 copy-start.2
  41.9 1.6 copy-start.4
  41.9 1.6 copy-start.1
  46.2 1.6 copy-start.3
  47.8 178.7 %all-reduce.4.cloned.1.call-start = ((), (), s32[]{:S(2)}) async-start(), calls=%async_computation | async-start | bytes 4718592 | tf_op jit(solution)/shard_map/psum | solution.py:83
  51.2 1.6 copy-start.6
Sparse Core Ops, SparseCore 0:
  47.9 75.1 all-reduce.5
  127.6 98.7 all-reduce.3
where the time goes:
time: 239 us; the launch traced here: 236 us
  waiting for transfers between devices  165 us (69%)
  blocking collectives  32.5 us (14%)
  between operations  14.9 us (6%)
  local copies, waits for them, and re-layouts  11.4 us (5%)
  matrix products  10.3 us (4%)
    psum x1, waiting for transfers between devices, body(): weight_grad = lax.psum(weight_term, ('query', 'car', 'replica'))  96.1 us
    unnamed x3, waiting for transfers between devices  69.1 us
    all_gather x1, blocking collectives, body(): kv_all = lax.all_gather(panel, ('query', 'car'), axis=0, tiled=True)  26.1 us
    unnamed x20, local copies, waits for them, and re-layouts  7.59 us
    psum x1, blocking collectives, body(): kv_mine = lax.psum(kv_part, 'replica')  6.4 us
  transfers between devices with their start and end apart: 2, of which 2 were waited for; matrix products, arithmetic and copies ran while one was open for 3% of the time, Pallas kernels for 0%

commit v1 on v0

--- a/solution.py
+++ b/solution.py
@@ -1,8 +1,11 @@
+import functools
 import math
 
 import jax
 import jax.numpy as jnp
 from jax import lax
+from jax.experimental import pallas as pl
+from jax.experimental.pallas import tpu as pltpu
 from jax.sharding import PartitionSpec as P
 
 D = 768
@@ -119,6 +122,336 @@
     return (grad_queries, kv_mine.reshape(1, anchors_each, 2 * D), weight_grad)
 
 
+TILE = 128
+GROUP = 4
+NT = (((1,), (1,)), ((), ()))
+TN = (((0,), (0,)), ((), ()))
+
+
+def dot(a, b, dims=(((1,), (0,)), ((), ()))):
+    return lax.dot_general(a, b, dims, preferred_element_type=jnp.float32)
+
+
+def fused_kernel(
+    xs, zs, counts, slots, kv, q_hbm, do_hbm, w_hbm, gq_hbm, gkv, gw_hbm,
+    q, do, w, pack, kvall, da, kbd, vbd, prob_s, ds_s, gq_v, gw_v, mb, pair, rs_out, rs_in, ag, dk,
+    in_sem, out_sem, kv_send, kv_recv, pair_sem, rs_send, rs_recv, ag_send, ag_recv,
+    fw_send, fw_recv, dk_sem,
+):
+    scale = HEAD_DIM ** (-0.5)
+    chips = xs * zs
+    groups = HEADS // GROUP
+    rows = q.shape[0]
+    grp, x, z, core = (lax.axis_index(a) for a in ("groups", "query", "car", "replica"))
+    me = x * zs + z
+    other = 1 - core
+    sibling = (grp, x, z, other)
+
+    def chip(offset):
+        n = lax.rem(me + offset, chips)
+        return n, (grp, n // zs, lax.rem(n, zs), core)
+
+    def remote(src, dst, send, recv, device):
+        return pltpu.make_async_remote_copy(
+            src_ref=src, dst_ref=dst, send_sem=send, recv_sem=recv, device_id=device,
+            device_id_type=pl.DeviceIdType.MESH,
+        )
+
+    loads = [
+        pltpu.make_async_copy(a, b, in_sem.at[i])
+        for i, (a, b) in enumerate(((do_hbm, do), (w_hbm, w), (q_hbm, q)))
+    ]
+    for load in loads:
+        load.start()
+
+    barrier = pltpu.get_barrier_semaphore()
+    for offset in range(1, chips):
+        pl.semaphore_signal(
+            barrier, inc=1, device_id=chip(offset)[1], device_id_type=pl.DeviceIdType.MESH
+        )
+    pl.semaphore_signal(barrier, inc=1, device_id=sibling, device_id_type=pl.DeviceIdType.MESH)
+
+    own_kv = kv[0].astype(jnp.float32)
+    for h in range(HEADS):
+        pack[h * 4 : h * 4 + 4, :HEAD_DIM] = own_kv[:, h * HEAD_DIM : (h + 1) * HEAD_DIM]
+        pack[h * 4 : h * 4 + 4, HEAD_DIM:] = own_kv[:, D + h * HEAD_DIM : D + (h + 1) * HEAD_DIM]
+    kvall[me] = pack[...].astype(jnp.bfloat16)
+
+    pl.semaphore_wait(barrier, chips)
+    kv_out = []
+    for offset in range(1, chips):
+        n, device = chip(offset)
+        copy = remote(
+            kvall.at[me], kvall.at[me], kv_send.at[offset - 1], kv_recv.at[offset - 1], device
+        )
+        copy.start()
+        kv_out.append(copy)
+
+    loads[0].wait()
+    loads[1].wait()
+    for g in range(groups):
+        cols = slice(g * 256, g * 256 + 256)
+        da[:, cols] = dot(do[...], w[cols, :], NT).astype(jnp.bfloat16)
+    loads[2].wait()
+
+    lane = lax.broadcasted_iota(jnp.int32, (8, rows), 1)
+    sub = lax.broadcasted_iota(jnp.int32, (8, rows), 0)
+    masks = []
+    for s in range(zs):
+        car = slots[s]
+        first = jnp.int32(0)
+        size = jnp.int32(0)
+        for c in range(counts.shape[1]):
+            first = first + jnp.where(c < car, counts[0, c], 0)
+            size = size + jnp.where(c == car, counts[0, c], 0)
+        masks.append((lane >= first) & (lane < first + size))
+
+    def swap(v, s):
+        return jnp.where((sub & s) == 0, pltpu.roll(v, 8 - s, 0), pltpu.roll(v, s, 0))
+
+    def over_four(v, op):
+        v = op(v, swap(v, 1))
+        return op(v, swap(v, 2))
+
+    def pick(full, xi, hp):
+        part = [full[(xi * zs + s) * 16 + hp * 8 : (xi * zs + s) * 16 + hp * 8 + 8, :] for s in range(zs)]
+        out = part[0]
+        for s in range(1, zs):
+            out = jnp.where(masks[s], part[s], out)
+        return out
+
+    for offset in range(1, chips):
+        n, device = chip(chips - offset)
+        remote(
+            kvall.at[n], kvall.at[n], kv_send.at[offset - 1], kv_recv.at[offset - 1], device
+        ).wait_recv()
+
+    krows = chips * 16
+    diag_row = lax.broadcasted_iota(jnp.int32, (krows, 256), 0) // 4 % GROUP
+    diag = diag_row == lax.broadcasted_iota(jnp.int32, (krows, 256), 1) // HEAD_DIM
+    half = lax.broadcasted_iota(jnp.int32, (krows, TILE), 1) < HEAD_DIM
+    key_tiles = []
+    for g in range(groups):
+        cols = slice(g * 256, g * 256 + 256)
+        both = kvall[:, g * 16 : g * 16 + 16, :].reshape(krows, TILE).astype(jnp.float32)
+        turned = pltpu.roll(both, HEAD_DIM, 1)
+        keys2 = jnp.where(half, both, turned)
+        vals2 = jnp.where(half, turned, both)
+        kd = jnp.where(diag, jnp.concatenate([keys2, keys2], axis=1), 0.0).astype(jnp.bfloat16)
+        vd = jnp.where(diag, jnp.concatenate([vals2, vals2], axis=1), 0.0).astype(jnp.bfloat16)
+        kbd[g] = kd
+        vbd[g] = vd
+        scores = dot(kd, q[:, cols], NT)
+        d_prob = dot(vd, da[:, cols], NT)
+        probs = [[None, None] for _ in range(xs)]
+        dss = [[None, None] for _ in range(xs)]
+        for hp in range(2):
+            sc = [pick(scores, xi, hp) * scale for xi in range(xs)]
+            dp = [pick(d_prob, xi, hp) for xi in range(xs)]
+            best = over_four(functools.reduce(jnp.maximum, sc), jnp.maximum)
+            wt = [jnp.exp(v - best) for v in sc]
+            total = over_four(functools.reduce(jnp.add, wt), jnp.add)
+            inv = 1.0 / total
+            pr = [v * inv for v in wt]
+            delta = over_four(functools.reduce(jnp.add, [a * b for a, b in zip(pr, dp)]), jnp.add)
+            for xi in range(xs):
+                probs[xi][hp] = pr[xi]
+                dss[xi][hp] = pr[xi] * (dp[xi] - delta)
+        for xi in range(xs):
+            for s in range(zs):
+                at = slice((xi * zs + s) * 16, (xi * zs + s) * 16 + 16)
+                mask = jnp.concatenate([masks[s], masks[s]], axis=0)
+                prob_s[at, :] = jnp.where(mask, jnp.concatenate(probs[xi], axis=0), 0.0).astype(
+                    jnp.bfloat16
+                )
+                ds_s[g, at, :] = jnp.where(mask, jnp.concatenate(dss[xi], axis=0), 0.0).astype(
+                    jnp.bfloat16
+                )
+        term = dot(prob_s[...], do[...]).astype(jnp.bfloat16)
+        for c in range(2):
+            for t in range(3):
+                at = (c * 3 + t) * TILE
+                mb[c, :, t * 48 + g * 16 : t * 48 + g * 16 + 16, :] = term[
+                    :, at : at + TILE
+                ].reshape(chips, 16, TILE)
+        d_key = jnp.where(diag, dot(ds_s[g], q[:, cols]), 0.0) * scale
+        d_key = d_key.reshape(chips, 2, 8, 256)
+        d_key = d_key[:, 0] + d_key[:, 1]
+        d_key = d_key + pltpu.roll(d_key, 4, 1)
+        key_tiles += [d_key[:, :, :TILE], d_key[:, :, TILE:]]
+    low = lax.broadcasted_iota(jnp.int32, (chips, 8, TILE), 1) < 4
+    for c in range(2):
+        a, b, e = key_tiles[3 * c : 3 * c + 3]
+        mb[c, :, 144:160, :] = jnp.concatenate(
+            [jnp.where(low, a, b), jnp.where(low, e, 0.0)], axis=1
+        ).astype(jnp.bfloat16)
+
+    swap_pair = remote(mb.at[other], pair, pair_sem.at[0], pair_sem.at[1], sibling)
+    swap_pair.start()
+    swap_pair.wait_recv()
+    rs_sent = []
+    for offset in range(1, chips):
+        n, device = chip(offset)
+        rs_out[offset - 1] = (
+            mb[core, n].astype(jnp.float32) + pair[n].astype(jnp.float32)
+        ).astype(jnp.bfloat16)
+        copy = remote(
+            rs_out.at[offset - 1], rs_in.at[offset - 1], rs_send.at[offset - 1],
+            rs_recv.at[offset - 1], device,
+        )
+        copy.start()
+        rs_sent.append(copy)
+
+    for g in range(groups):
+        cols = slice(g * 256, g * 256 + 256)
+        gq_v[:, cols] = (dot(ds_s[g], kbd[g], TN) * scale).astype(jnp.bfloat16)
+    stores = [pltpu.make_async_copy(gq_v, gq_hbm, out_sem.at[0])]
+    stores[0].start()
+
+    mine = mb[core, me].astype(jnp.float32) + pair[me].astype(jnp.float32)
+    for offset in range(1, chips):
+        rs_sent[offset - 1].wait_recv()
+        mine = mine + rs_in[offset - 1].astype(jnp.float32)
+    ag[core, me] = mine[:144].astype(jnp.bfloat16)
+    dk[core] = mine[144:]
+    ag_out = []
+    for offset in range(1, chips):
+        n, device = chip(offset)
+        copy = remote(
+            ag.at[core, me], ag.at[core, me], ag_send.at[offset - 1], ag_recv.at[offset - 1], device
+        )
+        copy.start()
+        ag_out.append(copy)
+    dk_copy = remote(dk.at[core], dk.at[core], dk_sem.at[0], dk_sem.at[1], sibling)
+    dk_copy.start()
+    fw_out = [remote(ag.at[core, me], ag.at[core, me], fw_send.at[0], fw_recv.at[0], sibling)]
+    fw_out[0].start()
+    for offset in range(1, chips):
+        n, device = chip(chips - offset)
+        remote(
+            ag.at[core, n], ag.at[core, n], ag_send.at[offset - 1], ag_recv.at[offset - 1], device
+        ).wait_recv()
+        copy = remote(
+            ag.at[core, n], ag.at[core, n], fw_send.at[offset], fw_recv.at[offset], sibling
+        )
+        copy.start()
+        fw_out.append(copy)
+
+    def arrived(offset):
+        n, _ = chip(chips - offset)
+        remote(
+            ag.at[other, n], ag.at[other, n], fw_send.at[offset], fw_recv.at[offset], sibling
+        ).wait_recv()
+
+    remote(dk.at[other], dk.at[other], dk_sem.at[0], dk_sem.at[1], sibling).wait_recv()
+    for c in range(2):
+        for t in range(3):
+            at = (c * 3 + t) * TILE
+            gkv[0, :, at : at + TILE] = dk[c, t * 4 : t * 4 + 4, :]
+    arrived(0)
+    for g in range(groups):
+        m_own = jnp.concatenate(
+            [ag[c, me, t * 48 + g * 16 : t * 48 + g * 16 + 16, :] for c in range(2) for t in range(3)],
+            axis=1,
+        )
+        r = jnp.where(diag[:16], dot(m_own, w[g * 256 : g * 256 + 256, :], NT), 0.0)
+        r = r[:8] + r[8:]
+        r = r + pltpu.roll(r, 4, 0)
+        gkv[0, :, D + g * 256 : D + g * 256 + 256] = r[:4]
+
+    for offset in range(1, chips):
+        arrived(offset)
+    for g in range(groups):
+        m_g = jnp.concatenate(
+            [
+                ag[c, :, t * 48 + g * 16 : t * 48 + g * 16 + 16, :].reshape(krows, TILE)
+                for c in range(2)
+                for t in range(3)
+            ],
+            axis=1,
+        )
+        part = slice(g * 256, g * 256 + 256)
+        gw_v[part, :] = dot(vbd[g], m_g, TN)
+        store = pltpu.make_async_copy(gw_v.at[part], gw_hbm.at[part], out_sem.at[1 + g])
+        store.start()
+        stores.append(store)
+    for copy in kv_out + [swap_pair] + rs_sent + ag_out + fw_out + [dk_copy]:
+        copy.wait_send()
+    for store in stores:
+        store.wait()
+
+
+def fused(xs, zs, query_heads, d_out, anchor_kv, point_counts, slot_car, out_weight):
+    chips = xs * zs
+    rows = query_heads.shape[0]
+    bf, f32 = jnp.bfloat16, jnp.float32
+    dma = lambda n: pltpu.SemaphoreType.DMA((n,))
+    smem = pl.BlockSpec(memory_space=pltpu.SMEM)
+    vmem = pl.BlockSpec(memory_space=pltpu.VMEM)
+    anywhere = pl.BlockSpec(memory_space=pl.ANY)
+    return pl.pallas_call(
+        functools.partial(fused_kernel, xs, zs),
+        out_shape=(
+            jax.ShapeDtypeStruct((rows, D), bf),
+            jax.ShapeDtypeStruct(anchor_kv.shape, f32),
+            jax.ShapeDtypeStruct((D, D), f32),
+        ),
+        in_specs=[smem, smem, vmem, anywhere, anywhere, anywhere],
+        out_specs=(anywhere, vmem, anywhere),
+        scratch_shapes=[
+            pltpu.VMEM((rows, D), bf),
+            pltpu.VMEM((rows, D), bf),
+            pltpu.VMEM((D, D), bf),
+            pltpu.VMEM((48, TILE), f32),
+            pltpu.VMEM((chips, 48, TILE), bf),
+            pltpu.VMEM((rows, D), bf),
+            pltpu.VMEM((3, chips * 16, 256), bf),
+            pltpu.VMEM((3, chips * 16, 256), bf),
+            pltpu.VMEM((chips * 16, rows), bf),
+            pltpu.VMEM((3, chips * 16, rows), bf),
+            pltpu.VMEM((rows, D), bf),
+            pltpu.VMEM((D, D), f32),
+            pltpu.VMEM((2, chips, 160, TILE), bf),
+            pltpu.VMEM((chips, 160, TILE), bf),
+            pltpu.VMEM((chips - 1, 160, TILE), bf),
+            pltpu.VMEM((chips - 1, 160, TILE), bf),
+            pltpu.VMEM((2, chips, 144, TILE), bf),
+            pltpu.VMEM((2, 16, TILE), f32),
+            dma(3),
+            dma(4),
+            dma(chips - 1),
+            dma(chips - 1),
+            dma(2),
+            dma(chips - 1),
+            dma(chips - 1),
+            dma(chips - 1),
+            dma(chips - 1),
+            dma(chips),
+            dma(chips),
+            dma(2),
+        ],
+        compiler_params=pltpu.CompilerParams(
+            collective_id=0, has_side_effects=True, vmem_limit_bytes=48 * 1024 * 1024
+        ),
+        cost_estimate=pl.CostEstimate(
+            flops=2 * rows * D * D * 3, bytes_accessed=8 * 1024 * 1024, transcendentals=rows * 96
+        ),
+    )(point_counts, slot_car, anchor_kv, query_heads, d_out, out_weight)
+
+
+def choose(mesh):
+    xs, zs, cores = mesh.shape["query"], mesh.shape["car"], mesh.shape["replica"]
+
+    def run(query_heads, d_out, anchor_kv, point_counts, slot_car, out_weight):
+        args = (query_heads, d_out, anchor_kv, point_counts, slot_car, out_weight)
+        few = xs * zs == 8 and cores == 2 and anchor_kv.shape[:2] == (1, 4)
+        if few and query_heads.shape[0] % TILE == 0:
+            return fused(xs, zs, *args)
+        return body(*args)
+
+    return run
+
+
 def solution(mesh):
     in_specs = (
         P(("groups", "query", "car", "replica"), None),
@@ -133,4 +466,4 @@
         P(("groups", "car"), "query", None),
         P("groups", None),
     )
-    return jax.shard_map(body, mesh=mesh, in_specs=in_specs, out_specs=out_specs, check_vma=False)
+    return jax.shard_map(choose(mesh), mesh=mesh, in_specs=in_specs, out_specs=out_specs, check_vma=False)

time: 239 us -> 41 us (0.17)
  waiting for transfers between devices: 165 us -> 0 us
  blocking collectives: 32.5 us -> 0 us
  Pallas kernels: 0 us -> 31.5 us
  between operations: 14.9 us -> 0.65 us
  matrix products: 10.3 us -> 0 us
  local copies, waits for them, and re-layouts: 11.4 us -> 8.44 us
    psum x1 -> x0, waiting for transfers between devices: 96.1 us -> none  [body(): weight_grad = lax.psum(weight_term, ('query', 'car', 'replica'))]
    unnamed x3 -> x0, waiting for transfers between devices: 69.1 us -> none
    pallas_call x0 -> x1, Pallas kernels: none -> 31.5 us  [fused(): pl.pallas_call(functools.partial(fused_kernel, xs, zs), out_shape=(jax.Sh...]
    all_gather x1 -> x0, blocking collectives: 26.1 us -> none  [body(): kv_all = lax.all_gather(panel, ('query', 'car'), axis=0, tiled=True)]
    dot_general x8 -> x0, matrix products: 10.3 us -> none  [the longest x1 3.32 us: body(): lax.dot_general(attended, d_out, (((0,), (0,)), ((), ())), preferred_elem...]
    psum x1 -> x0, blocking collectives: 6.4 us -> none  [body(): kv_mine = lax.psum(kv_part, 'replica')]
    unnamed x20 -> x15, local copies, waits for them, and re-layouts: 7.59 us -> 8.44 us
  transfers between devices with their start and end apart: 2 -> 0, of which waited for: 2 -> 0; matrix products, arithmetic and copies ran while one was open for 3% -> 0% of each run, Pallas kernels for 0% -> 0%
where the time goes in v1:
time: 41 us; the launch traced here: 40.6 us
  Pallas kernels  31.5 us (77%)
  local copies, waits for them, and re-layouts  8.44 us (21%)
  between operations  0.65 us (2%)
    pallas_call x1, Pallas kernels, fused(): pl.pallas_call(functools.partial(fused_kernel, xs, zs), out_shape=(jax.Sh...  31.5 us
    unnamed x15, local copies, waits for them, and re-layouts  8.44 us

profile of v1, /device:TPU:1, one launch (start us, length us, event | category | flops | bytes accessed | tf_op | source)
XLA Modules:
  0.0 40.6 jit_solution(4927515978377293331)
XLA Ops:
  0.6 0.0 copy-start
  0.6 1.3 %copy-done = bf16[768,768]{1,0:T(8,128)(2,1)S(1)} copy-done((bf16[768,768]{1,0:T(8,128)(2,1)S(1)}, bf16[768,768]{1,0:T(8,128)(2,1)}, u32[]{:S(2)}) %copy-start) | copy-done | bytes 1179672
  1.9 0.0 copy-start.1
  1.9 1.1 %copy-done.1 = bf16[512,768]{1,0:T(8,128)(2,1)S(1)} copy-done((bf16[512,768]{1,0:T(8,128)(2,1)S(1)}, bf16[512,768]{1,0:T(8,128)(2,1)}, u32[]{:S(2)}) %copy-start.1) | copy-done | bytes 786456
  3.0 0.0 copy-start.2
  3.0 1.1 %copy-done.2 = bf16[512,768]{1,0:T(8,128)(2,1)S(1)} copy-done((bf16[512,768]{1,0:T(8,128)(2,1)S(1)}, bf16[512,768]{1,0:T(8,128)(2,1)}, u32[]{:S(2)}) %copy-start.2) | copy-done | bytes 786456
  4.2 0.0 copy-start.3
  4.2 0.7 %copy-done.3 = bf16[1,4,1536]{2,1,0:T(4,128)(2,1)S(1)} copy-done((bf16[1,4,1536]{2,1,0:T(4,128)(2,1)S(1)}, bf16[1,4,1536]{2,1,0:T(4,128)(2,1)}, u32[]{:S(2)}) %copy-start.3) | copy-done | bytes 12312
  4.9 0.0 copy-start.4
  4.9 0.7 %copy-done.4 = s32[1,4]{1,0:T(1,128)S(1)} copy-done((s32[1,4]{1,0:T(1,128)S(1)}, s32[1,4]{1,0:T(1,128)}, u32[]{:S(2)}) %copy-start.4) | copy-done | bytes 40
  5.5 0.0 copy-start.5
  5.5 0.7 %copy-done.5 = s32[4]{0:T(128)S(1)} copy-done((s32[4]{0:T(128)S(1)}, s32[4]{0:T(128)}, u32[]{:S(2)}) %copy-start.5) | copy-done | bytes 40
  6.2 31.5 %shard_map.85 = (bf16[512,768]{1,0:T(8,128)(2,1)S(1)}, f32[1,4,1536]{2,1,0:T(4,128)S(1)}, f32[768,768]{1,0:T(8,128)S(1)}) custom-call(s32[1,4]{1,0:T(1,128)S(1)} %copy-done.4, s32[4]{0:T(128)S(1)} %copy-done.5, bf16[1,4,1536]{2,1,0:T(4,128)(2,1)S(1)} %copy-done.3, bf16[512,768]{1,0:T(8,128)(2,1)S(1)} %copy-done.1, bf16[512,768]{1,0:T(8,128)(2,1)S(1)} %copy-done.2, ...), custom_call_target="tpu_custom_call" | custom-call | flops 1811939328 | bytes 8388608 | tf_op jit(solution)/shard_map/pallas_call | solution.py:392
  37.7 0.9 %copy.12 = bf16[512,768]{1,0:T(8,128)(2,1)} copy(bf16[512,768]{1,0:T(8,128)(2,1)S(1)} %get-tuple-element.6) | data formatting | bytes 1572864
  38.6 0.6 %copy.13 = f32[1,4,1536]{2,1,0:T(4,128)} copy(f32[1,4,1536]{2,1,0:T(4,128)S(1)} %get-tuple-element.7) | data formatting | bytes 49152
  39.2 1.4 %copy.14 = f32[768,768]{1,0:T(8,128)} copy(f32[768,768]{1,0:T(8,128)S(1)} %get-tuple-element.8) | data formatting | bytes 4718592
Async XLA Ops:
  0.6 1.3 %copy-start = (bf16[768,768]{1,0:T(8,128)(2,1)S(1)}, bf16[768,768]{1,0:T(8,128)(2,1)}, u32[]{:S(2)}) copy-start(bf16[768,768]{1,0:T(8,128)(2,1)} %w_hbm.1) | copy-start | bytes 3538948
  1.9 1.1 %copy-start.1 = (bf16[512,768]{1,0:T(8,128)(2,1)S(1)}, bf16[512,768]{1,0:T(8,128)(2,1)}, u32[]{:S(2)}) copy-start(bf16[512,768]{1,0:T(8,128)(2,1)} %q_hbm.1) | copy-start | bytes 2359300
  3.0 1.1 %copy-start.2 = (bf16[512,768]{1,0:T(8,128)(2,1)S(1)}, bf16[512,768]{1,0:T(8,128)(2,1)}, u32[]{:S(2)}) copy-start(bf16[512,768]{1,0:T(8,128)(2,1)} %do_hbm.1) | copy-start | bytes 2359300
  4.2 0.7 %copy-start.3 = (bf16[1,4,1536]{2,1,0:T(4,128)(2,1)S(1)}, bf16[1,4,1536]{2,1,0:T(4,128)(2,1)}, u32[]{:S(2)}) copy-start(bf16[1,4,1536]{2,1,0:T(4,128)(2,1)} %kv.1) | copy-start | bytes 36868
  4.9 0.7 %copy-start.4 = (s32[1,4]{1,0:T(1,128)S(1)}, s32[1,4]{1,0:T(1,128)}, u32[]{:S(2)}) copy-start(s32[1,4]{1,0:T(1,128)} %counts.1) | copy-start | bytes 52
  5.5 0.7 %copy-start.5 = (s32[4]{0:T(128)S(1)}, s32[4]{0:T(128)}, u32[]{:S(2)}) copy-start(s32[4]{0:T(128)} %slots.1) | copy-start | bytes 52

commit v2 on v1

--- a/solution.py
+++ b/solution.py
@@ -133,10 +133,10 @@
 
 
 def fused_kernel(
-    xs, zs, counts, slots, kv, q_hbm, do_hbm, w_hbm, gq_hbm, gkv, gw_hbm,
-    q, do, w, pack, kvall, da, kbd, vbd, prob_s, ds_s, gq_v, gw_v, mb, pair, rs_out, rs_in, ag, dk,
-    in_sem, out_sem, kv_send, kv_recv, pair_sem, rs_send, rs_recv, ag_send, ag_recv,
-    fw_send, fw_recv, dk_sem,
+    xs, zs, counts_hbm, slots_hbm, kv, q_hbm, do_hbm, w_hbm, ag_hbm, gkv_hbm, kbd_hbm, vbd_hbm, ds_hbm,
+    counts, slots, q, do, w, pack, kvall, da, kbd, vbd, prob_s, ds_s, mb, pair, x_out, x_in, z_out,
+    z_in, ag, dk, gkv, in_sem, kv_send, kv_recv, pair_sem, x_send, x_recv, z_send, z_recv, agz_send,
+    agz_recv, agx_send, agx_recv, fw_send, fw_recv, dk_sem, out_sem, piece_sem,
 ):
     scale = HEAD_DIM ** (-0.5)
     chips = xs * zs
@@ -146,6 +146,17 @@
     me = x * zs + z
     other = 1 - core
     sibling = (grp, x, z, other)
+    across = (grp, 1 - x, z, core)
+    stores = []
+
+    def store(src, dst, sem):
+        copy = pltpu.make_async_copy(src, dst, sem)
+        copy.start()
+        stores.append(copy)
+
+    def along(offset):
+        to = lax.rem(z + offset, zs)
+        return to, (grp, x, to, core)
 
     def chip(offset):
         n = lax.rem(me + offset, chips)
@@ -159,7 +170,7 @@
 
     loads = [
         pltpu.make_async_copy(a, b, in_sem.at[i])
-        for i, (a, b) in enumerate(((do_hbm, do), (w_hbm, w), (q_hbm, q)))
+        for i, (a, b) in enumerate(((do_hbm, do), (w_hbm, w), (q_hbm, q), (counts_hbm, counts), (slots_hbm, slots)))
     ]
     for load in loads:
         load.start()
@@ -192,7 +203,8 @@
     for g in range(groups):
         cols = slice(g * 256, g * 256 + 256)
         da[:, cols] = dot(do[...], w[cols, :], NT).astype(jnp.bfloat16)
-    loads[2].wait()
+    for load in loads[2:]:
+        load.wait()
 
     lane = lax.broadcasted_iota(jnp.int32, (8, rows), 1)
     sub = lax.broadcasted_iota(jnp.int32, (8, rows), 0)
@@ -288,66 +300,95 @@
 
     swap_pair = remote(mb.at[other], pair, pair_sem.at[0], pair_sem.at[1], sibling)
     swap_pair.start()
+    store(kbd, kbd_hbm, out_sem.at[0])
+    store(vbd, vbd_hbm, out_sem.at[1])
+    store(ds_s, ds_hbm, out_sem.at[2])
     swap_pair.wait_recv()
-    rs_sent = []
-    for offset in range(1, chips):
-        n, device = chip(offset)
-        rs_out[offset - 1] = (
-            mb[core, n].astype(jnp.float32) + pair[n].astype(jnp.float32)
+    x_sent, z_sent = [], []
+    order = list(range(1, zs)) + [0]
+
+    def summed(n):
+        return mb[core, n].astype(jnp.float32) + pair[n].astype(jnp.float32)
+
+    for o in order:
+        x_out[o] = summed((1 - x) * zs + along(o)[0]).astype(jnp.bfloat16)
+        copy = remote(x_out.at[o], x_in.at[o], x_send.at[o], x_recv.at[o], across)
+        copy.start()
+        x_sent.append(copy)
+    for i, o in enumerate(order[:-1]):
+        to, device = along(o)
+        x_sent[i].wait_recv()
+        z_out[o - 1] = (
+            summed(x * zs + to) + x_in[o].astype(jnp.float32)
         ).astype(jnp.bfloat16)
         copy = remote(
-            rs_out.at[offset - 1], rs_in.at[offset - 1], rs_send.at[offset - 1],
-            rs_recv.at[offset - 1], device,
-        )
-        copy.start()
-        rs_sent.append(copy)
-
-    for g in range(groups):
-        cols = slice(g * 256, g * 256 + 256)
-        gq_v[:, cols] = (dot(ds_s[g], kbd[g], TN) * scale).astype(jnp.bfloat16)
-    stores = [pltpu.make_async_copy(gq_v, gq_hbm, out_sem.at[0])]
-    stores[0].start()
-
-    mine = mb[core, me].astype(jnp.float32) + pair[me].astype(jnp.float32)
-    for offset in range(1, chips):
-        rs_sent[offset - 1].wait_recv()
-        mine = mine + rs_in[offset - 1].astype(jnp.float32)
+            z_out.at[o - 1], z_in.at[o - 1], z_send.at[o - 1], z_recv.at[o - 1], device
+        )
+        copy.start()
+        z_sent.append(copy)
+    x_sent[-1].wait_recv()
+    mine = summed(me) + x_in[0].astype(jnp.float32)
+    for copy in z_sent:
+        copy.wait_recv()
+    for o in range(1, zs):
+        mine = mine + z_in[o - 1].astype(jnp.float32)
     ag[core, me] = mine[:144].astype(jnp.bfloat16)
     dk[core] = mine[144:]
-    ag_out = []
-    for offset in range(1, chips):
-        n, device = chip(offset)
+    agz_out, agx_out, fw_out = [], [], []
+    for o in range(1, zs):
         copy = remote(
-            ag.at[core, me], ag.at[core, me], ag_send.at[offset - 1], ag_recv.at[offset - 1], device
-        )
-        copy.start()
-        ag_out.append(copy)
+            ag.at[core, me], ag.at[core, me], agz_send.at[o - 1], agz_recv.at[o - 1], along(o)[1]
+        )
+        copy.start()
+        agz_out.append(copy)
+
+    def to_across(o):
+        n = x * zs + along(zs - o)[0]
+        copy = remote(ag.at[core, n], ag.at[core, n], agx_send.at[o], agx_recv.at[o], across)
+        copy.start()
+        agx_out.append(copy)
+
+    def piece(i):
+        return (x if i < zs else 1 - x) * zs + along(zs - i % zs)[0]
+
+    def to_sibling(i):
+        n = piece(i)
+        copy = remote(ag.at[core, n], ag.at[core, n], fw_send.at[i], fw_recv.at[i], sibling)
+        copy.start()
+        fw_out.append(copy)
+        store(ag.at[core, n], ag_hbm.at[core, n], piece_sem.at[0, i])
+
+    def arrived(i):
+        n = piece(i)
+        remote(
+            ag.at[other, n], ag.at[other, n], fw_send.at[i], fw_recv.at[i], sibling
+        ).wait_recv()
+        store(ag.at[other, n], ag_hbm.at[other, n], piece_sem.at[1, i])
+
+    to_across(0)
     dk_copy = remote(dk.at[core], dk.at[core], dk_sem.at[0], dk_sem.at[1], sibling)
     dk_copy.start()
-    fw_out = [remote(ag.at[core, me], ag.at[core, me], fw_send.at[0], fw_recv.at[0], sibling)]
-    fw_out[0].start()
-    for offset in range(1, chips):
-        n, device = chip(chips - offset)
+    to_sibling(0)
+    for o in range(1, zs):
+        n = piece(o)
         remote(
-            ag.at[core, n], ag.at[core, n], ag_send.at[offset - 1], ag_recv.at[offset - 1], device
+            ag.at[core, n], ag.at[core, n], agz_send.at[o - 1], agz_recv.at[o - 1], along(o)[1]
         ).wait_recv()
-        copy = remote(
-            ag.at[core, n], ag.at[core, n], fw_send.at[offset], fw_recv.at[offset], sibling
-        )
-        copy.start()
-        fw_out.append(copy)
-
-    def arrived(offset):
-        n, _ = chip(chips - offset)
+        to_across(o)
+        to_sibling(o)
+
+    def from_across(o):
+        n = piece(zs + o)
         remote(
-            ag.at[other, n], ag.at[other, n], fw_send.at[offset], fw_recv.at[offset], sibling
+            ag.at[core, n], ag.at[core, n], agx_send.at[o], agx_recv.at[o], across
         ).wait_recv()
+        to_sibling(zs + o)
 
     remote(dk.at[other], dk.at[other], dk_sem.at[0], dk_sem.at[1], sibling).wait_recv()
     for c in range(2):
         for t in range(3):
             at = (c * 3 + t) * TILE
-            gkv[0, :, at : at + TILE] = dk[c, t * 4 : t * 4 + 4, :]
+            gkv[:, at : at + TILE] = dk[c, t * 4 : t * 4 + 4, :]
     arrived(0)
     for g in range(groups):
         m_own = jnp.concatenate(
@@ -357,10 +398,43 @@
         r = jnp.where(diag[:16], dot(m_own, w[g * 256 : g * 256 + 256, :], NT), 0.0)
         r = r[:8] + r[8:]
         r = r + pltpu.roll(r, 4, 0)
-        gkv[0, :, D + g * 256 : D + g * 256 + 256] = r[:4]
-
-    for offset in range(1, chips):
-        arrived(offset)
+        gkv[:, D + g * 256 : D + g * 256 + 256] = r[:4]
+    store(gkv, gkv_hbm.at[0], out_sem.at[3])
+
+    for o in range(zs):
+        from_across(o)
+    for i in range(1, 2 * zs):
+        arrived(i)
+    for copy in kv_out + [swap_pair] + x_sent + z_sent + agz_out + agx_out + fw_out + [dk_copy]:
+        copy.wait_send()
+    for copy in stores:
+        copy.wait()
+
+
+def last_kernel(
+    ag_hbm, gkv_hbm, kbd_hbm, vbd_hbm, ds_hbm, gq_out, gkv_out, gw_out,
+    ag, kbd, vbd, ds_s, gq, gw, in_sem, out_sem,
+):
+    scale = HEAD_DIM ** (-0.5)
+    krows = kbd.shape[1]
+    groups = HEADS // GROUP
+    loads = [
+        pltpu.make_async_copy(a, b, in_sem.at[i])
+        for i, (a, b) in enumerate(((ds_hbm, ds_s), (kbd_hbm, kbd), (vbd_hbm, vbd), (ag_hbm, ag)))
+    ]
+    for load in loads:
+        load.start()
+    stores = [pltpu.make_async_copy(gkv_hbm, gkv_out, out_sem.at[0])]
+    stores[0].start()
+    loads[0].wait()
+    loads[1].wait()
+    for g in range(groups):
+        cols = slice(g * 256, g * 256 + 256)
+        gq[:, cols] = (dot(ds_s[g], kbd[g], TN) * scale).astype(jnp.bfloat16)
+    stores.append(pltpu.make_async_copy(gq, gq_out, out_sem.at[1]))
+    stores[1].start()
+    loads[2].wait()
+    loads[3].wait()
     for g in range(groups):
         m_g = jnp.concatenate(
             [
@@ -371,14 +445,11 @@
             axis=1,
         )
         part = slice(g * 256, g * 256 + 256)
-        gw_v[part, :] = dot(vbd[g], m_g, TN)
-        store = pltpu.make_async_copy(gw_v.at[part], gw_hbm.at[part], out_sem.at[1 + g])
-        store.start()
-        stores.append(store)
-    for copy in kv_out + [swap_pair] + rs_sent + ag_out + fw_out + [dk_copy]:
-        copy.wait_send()
-    for store in stores:
-        store.wait()
+        gw[part, :] = dot(vbd[g], m_g, TN)
+        stores.append(pltpu.make_async_copy(gw.at[part], gw_out.at[part], out_sem.at[2 + g]))
+        stores[-1].start()
+    for copy in stores:
+        copy.wait()
 
 
 def fused(xs, zs, query_heads, d_out, anchor_kv, point_counts, slot_car, out_weight):
@@ -386,57 +457,95 @@
     rows = query_heads.shape[0]
     bf, f32 = jnp.bfloat16, jnp.float32
     dma = lambda n: pltpu.SemaphoreType.DMA((n,))
-    smem = pl.BlockSpec(memory_space=pltpu.SMEM)
+    hbm = pl.BlockSpec(memory_space=pltpu.HBM)
     vmem = pl.BlockSpec(memory_space=pltpu.VMEM)
-    anywhere = pl.BlockSpec(memory_space=pl.ANY)
-    return pl.pallas_call(
+    limit = 60 * 1024 * 1024
+    half_shape = (chips, 160, TILE)
+    kd_shape = (3, chips * 16, 256)
+    ds_shape = (3, chips * 16, rows)
+    ag_shape = (2, chips, 144, TILE)
+    mids = pl.pallas_call(
         functools.partial(fused_kernel, xs, zs),
         out_shape=(
-            jax.ShapeDtypeStruct((rows, D), bf),
+            jax.ShapeDtypeStruct(ag_shape, bf),
             jax.ShapeDtypeStruct(anchor_kv.shape, f32),
-            jax.ShapeDtypeStruct((D, D), f32),
+            jax.ShapeDtypeStruct(kd_shape, bf),
+            jax.ShapeDtypeStruct(kd_shape, bf),
+            jax.ShapeDtypeStruct(ds_shape, bf),
         ),
-        in_specs=[smem, smem, vmem, anywhere, anywhere, anywhere],
-        out_specs=(anywhere, vmem, anywhere),
+        in_specs=[hbm, hbm, vmem, hbm, hbm, hbm],
+        out_specs=(hbm,) * 5,
         scratch_shapes=[
+            pltpu.SMEM(point_counts.shape, jnp.int32),
+            pltpu.SMEM(slot_car.shape, jnp.int32),
             pltpu.VMEM((rows, D), bf),
             pltpu.VMEM((rows, D), bf),
             pltpu.VMEM((D, D), bf),
             pltpu.VMEM((48, TILE), f32),
             pltpu.VMEM((chips, 48, TILE), bf),
             pltpu.VMEM((rows, D), bf),
-            pltpu.VMEM((3, chips * 16, 256), bf),
-            pltpu.VMEM((3, chips * 16, 256), bf),
+            pltpu.VMEM(kd_shape, bf),
+            pltpu.VMEM(kd_shape, bf),
             pltpu.VMEM((chips * 16, rows), bf),
-            pltpu.VMEM((3, chips * 16, rows), bf),
-            pltpu.VMEM((rows, D), bf),
-            pltpu.VMEM((D, D), f32),
-            pltpu.VMEM((2, chips, 160, TILE), bf),
-            pltpu.VMEM((chips, 160, TILE), bf),
-            pltpu.VMEM((chips - 1, 160, TILE), bf),
-            pltpu.VMEM((chips - 1, 160, TILE), bf),
-            pltpu.VMEM((2, chips, 144, TILE), bf),
+            pltpu.VMEM(ds_shape, bf),
+            pltpu.VMEM((2,) + half_shape, bf),
+            pltpu.VMEM(half_shape, bf),
+            pltpu.VMEM((zs, 160, TILE), bf),
+            pltpu.VMEM((zs, 160, TILE), bf),
+            pltpu.VMEM((zs - 1, 160, TILE), bf),
+            pltpu.VMEM((zs - 1, 160, TILE), bf),
+            pltpu.VMEM(ag_shape, bf),
             pltpu.VMEM((2, 16, TILE), f32),
-            dma(3),
-            dma(4),
+            pltpu.VMEM(anchor_kv.shape[1:], f32),
+            dma(5),
             dma(chips - 1),
             dma(chips - 1),
             dma(2),
-            dma(chips - 1),
-            dma(chips - 1),
-            dma(chips - 1),
-            dma(chips - 1),
+            dma(zs),
+            dma(zs),
+            dma(zs - 1),
+            dma(zs - 1),
+            dma(zs - 1),
+            dma(zs - 1),
+            dma(zs),
+            dma(zs),
             dma(chips),
             dma(chips),
             dma(2),
+            dma(4),
+            pltpu.SemaphoreType.DMA((2, chips)),
         ],
         compiler_params=pltpu.CompilerParams(
-            collective_id=0, has_side_effects=True, vmem_limit_bytes=48 * 1024 * 1024
+            collective_id=0, has_side_effects=True, vmem_limit_bytes=limit
         ),
         cost_estimate=pl.CostEstimate(
-            flops=2 * rows * D * D * 3, bytes_accessed=8 * 1024 * 1024, transcendentals=rows * 96
+            flops=2 * rows * D * D * 2, bytes_accessed=5 * 1024 * 1024, transcendentals=rows * 96
         ),
     )(point_counts, slot_car, anchor_kv, query_heads, d_out, out_weight)
+    return pl.pallas_call(
+        last_kernel,
+        out_shape=(
+            jax.ShapeDtypeStruct((rows, D), bf),
+            jax.ShapeDtypeStruct(anchor_kv.shape, f32),
+            jax.ShapeDtypeStruct((D, D), f32),
+        ),
+        in_specs=[hbm] * 5,
+        out_specs=(hbm,) * 3,
+        scratch_shapes=[
+            pltpu.VMEM(ag_shape, bf),
+            pltpu.VMEM(kd_shape, bf),
+            pltpu.VMEM(kd_shape, bf),
+            pltpu.VMEM(ds_shape, bf),
+            pltpu.VMEM((rows, D), bf),
+            pltpu.VMEM((D, D), f32),
+            dma(4),
+            dma(5),
+        ],
+        compiler_params=pltpu.CompilerParams(vmem_limit_bytes=limit),
+        cost_estimate=pl.CostEstimate(
+            flops=2 * rows * D * D, bytes_accessed=5 * 1024 * 1024, transcendentals=0
+        ),
+    )(*mids)
 
 
 def choose(mesh):

time: 41 us -> 34.9 us (0.85)
  local copies, waits for them, and re-layouts: 8.44 us -> 0 us
  Pallas kernels: 31.5 us -> 34 us
    unnamed x15 -> x0, local copies, waits for them, and re-layouts: 8.44 us -> none
    pallas_call x0 -> x1, Pallas kernels: none -> 3.26 us  [fused(): pl.pallas_call(last_kernel, out_shape=(jax.ShapeDtypeStruct((rows, D), bf...]
    pallas_call x1, Pallas kernels: 31.5 us -> 30.7 us  [fused(): pl.pallas_call(functools.partial(fused_kernel, xs, zs), out_shape=(jax.Sh...]
where the time goes in v2:
time: 34.9 us; the launch traced here: 34.6 us
  Pallas kernels  34 us (97%)
  between operations  0.64 us (2%)
    pallas_call x1, Pallas kernels, fused(): pl.pallas_call(functools.partial(fused_kernel, xs, zs), out_shape=(jax.Sh...  30.7 us
    pallas_call x1, Pallas kernels, fused(): pl.pallas_call(last_kernel, out_shape=(jax.ShapeDtypeStruct((rows, D), bf...  3.26 us

profile of v2, /device:TPU:1, one launch (start us, length us, event | category | flops | bytes accessed | tf_op | source)
XLA Modules:
  0.0 34.6 jit_solution(15462362467013601811)
XLA Ops:
  0.6 30.7 %shard_map.85 = (bf16[2,8,144,128]{3,2,1,0:T(8,128)(2,1)}, f32[1,4,1536]{2,1,0:T(4,128)}, bf16[3,128,256]{2,1,0:T(8,128)(2,1)}, bf16[3,128,256]{2,1,0:T(8,128)(2,1)}, bf16[3,128,512]{2,1,0:T(8,128)(2,1)}) custom-call(s32[1,4]{1,0:T(1,128)} %counts_hbm.1, s32[4]{0:T(128)} %slots_hbm.1, bf16[1,4,1536]{2,1,0:T(4,128)(2,1)} %kv.1, bf16[512,768]{1,0:T(8,128)(2,1)} %q_hbm.1, ...), custom_call_target="tpu_custom_call" | custom-call | flops 1207959552 | bytes 5242880 | tf_op jit(solution)/shard_map/pallas_call | solution.py:467
  31.4 3.3 %shard_map.86 = (bf16[512,768]{1,0:T(8,128)(2,1)}, f32[1,4,1536]{2,1,0:T(4,128)}, f32[768,768]{1,0:T(8,128)}) custom-call(bf16[2,8,144,128]{3,2,1,0:T(8,128)(2,1)} %get-tuple-element.8.ag_hbm, f32[1,4,1536]{2,1,0:T(4,128)} %get-tuple-element.9.gkv_hbm, bf16[3,128,256]{2,1,0:T(8,128)(2,1)} %get-tuple-element.10.kbd_hbm, ...), custom_call_target="tpu_custom_call" | custom-call | flops 603979776 | bytes 5242880 | tf_op jit(solution)/shard_map/pallas_call | solution.py:525

commit v3 on v2

--- a/solution.py
+++ b/solution.py
@@ -136,7 +136,7 @@
     xs, zs, counts_hbm, slots_hbm, kv, q_hbm, do_hbm, w_hbm, ag_hbm, gkv_hbm, kbd_hbm, vbd_hbm, ds_hbm,
     counts, slots, q, do, w, pack, kvall, da, kbd, vbd, prob_s, ds_s, mb, pair, x_out, x_in, z_out,
     z_in, ag, dk, gkv, in_sem, kv_send, kv_recv, pair_sem, x_send, x_recv, z_send, z_recv, agz_send,
-    agz_recv, agx_send, agx_recv, fw_send, fw_recv, dk_sem, out_sem, piece_sem,
+    agz_recv, agx_send, agx_recv, fw_send, fw_recv, dk_sem, out_sem,
 ):
     scale = HEAD_DIM ** (-0.5)
     chips = xs * zs
@@ -155,12 +155,19 @@
         stores.append(copy)
 
     def along(offset):
-        to = lax.rem(z + offset, zs)
+        to = line[offset % zs]
         return to, (grp, x, to, core)
 
+    line = [z] + [lax.rem(z + offset, zs) for offset in range(1, zs)]
+
     def chip(offset):
-        n = lax.rem(me + offset, chips)
-        return n, (grp, n // zs, lax.rem(n, zs), core)
+        to_x = x if offset % chips < zs else 1 - x
+        to_z = line[offset % zs]
+        return to_x * zs + to_z, (grp, to_x, to_z, core)
+
+    def source(offset):
+        to_x = x if offset < zs else 1 - x
+        return to_x * zs + line[(zs - offset % zs) % zs]
 
     def remote(src, dst, send, recv, device):
         return pltpu.make_async_remote_copy(
@@ -233,7 +240,7 @@
         return out
 
     for offset in range(1, chips):
-        n, device = chip(chips - offset)
+        n, device = source(offset), across
         remote(
             kvall.at[n], kvall.at[n], kv_send.at[offset - 1], kv_recv.at[offset - 1], device
         ).wait_recv()
@@ -298,98 +305,116 @@
             [jnp.where(low, a, b), jnp.where(low, e, 0.0)], axis=1
         ).astype(jnp.bfloat16)
 
-    swap_pair = remote(mb.at[other], pair, pair_sem.at[0], pair_sem.at[1], sibling)
-    swap_pair.start()
+    parts = (slice(0, 80), slice(80, 160))
+    swaps = []
+    for p, rs in enumerate(parts):
+        copy = remote(
+            mb.at[other, :, rs], pair.at[:, rs], pair_sem.at[0, p], pair_sem.at[1, p], sibling
+        )
+        copy.start()
+        swaps.append(copy)
     store(kbd, kbd_hbm, out_sem.at[0])
     store(vbd, vbd_hbm, out_sem.at[1])
     store(ds_s, ds_hbm, out_sem.at[2])
-    swap_pair.wait_recv()
-    x_sent, z_sent = [], []
     order = list(range(1, zs)) + [0]
-
-    def summed(n):
-        return mb[core, n].astype(jnp.float32) + pair[n].astype(jnp.float32)
-
-    for o in order:
-        x_out[o] = summed((1 - x) * zs + along(o)[0]).astype(jnp.bfloat16)
-        copy = remote(x_out.at[o], x_in.at[o], x_send.at[o], x_recv.at[o], across)
-        copy.start()
-        x_sent.append(copy)
-    for i, o in enumerate(order[:-1]):
-        to, device = along(o)
-        x_sent[i].wait_recv()
-        z_out[o - 1] = (
-            summed(x * zs + to) + x_in[o].astype(jnp.float32)
-        ).astype(jnp.bfloat16)
-        copy = remote(
-            z_out.at[o - 1], z_in.at[o - 1], z_send.at[o - 1], z_recv.at[o - 1], device
-        )
-        copy.start()
-        z_sent.append(copy)
-    x_sent[-1].wait_recv()
-    mine = summed(me) + x_in[0].astype(jnp.float32)
-    for copy in z_sent:
-        copy.wait_recv()
-    for o in range(1, zs):
-        mine = mine + z_in[o - 1].astype(jnp.float32)
-    ag[core, me] = mine[:144].astype(jnp.bfloat16)
-    dk[core] = mine[144:]
-    agz_out, agx_out, fw_out = [], [], []
-    for o in range(1, zs):
-        copy = remote(
-            ag.at[core, me], ag.at[core, me], agz_send.at[o - 1], agz_recv.at[o - 1], along(o)[1]
-        )
-        copy.start()
-        agz_out.append(copy)
-
-    def to_across(o):
+    x_sent, z_sent, agz_out, agx_out, fw_out = [], [], [], [], []
+
+    def summed(n, rs):
+        return mb[core, n, rs].astype(jnp.float32) + pair[n, rs].astype(jnp.float32)
+
+    for p, rs in enumerate(parts):
+        swaps[p].wait_recv()
+        for o in order:
+            x_out[o, rs] = summed((1 - x) * zs + along(o)[0], rs).astype(jnp.bfloat16)
+            copy = remote(
+                x_out.at[o, rs], x_in.at[o, rs], x_send.at[p, o], x_recv.at[p, o], across
+            )
+            copy.start()
+            x_sent.append(copy)
+    for p, rs in enumerate(parts):
+        for i, o in enumerate(order[:-1]):
+            to, device = along(o)
+            x_sent[p * zs + i].wait_recv()
+            z_out[o - 1, rs] = (
+                summed(x * zs + to, rs) + x_in[o, rs].astype(jnp.float32)
+            ).astype(jnp.bfloat16)
+            copy = remote(
+                z_out.at[o - 1, rs], z_in.at[o - 1, rs], z_send.at[p, o - 1],
+                z_recv.at[p, o - 1], device,
+            )
+            copy.start()
+            z_sent.append(copy)
+
+    def rows_of(p):
+        return slice(0, 80) if p == 0 else slice(80, 144)
+
+    def to_across(p, o):
         n = x * zs + along(zs - o)[0]
-        copy = remote(ag.at[core, n], ag.at[core, n], agx_send.at[o], agx_recv.at[o], across)
+        at = ag.at[core, n, rows_of(p)]
+        copy = remote(at, at, agx_send.at[p, o], agx_recv.at[p, o], across)
         copy.start()
         agx_out.append(copy)
 
     def piece(i):
         return (x if i < zs else 1 - x) * zs + along(zs - i % zs)[0]
 
-    def to_sibling(i):
+    def to_sibling(p, i):
         n = piece(i)
-        copy = remote(ag.at[core, n], ag.at[core, n], fw_send.at[i], fw_recv.at[i], sibling)
+        at = ag.at[core, n, rows_of(p)]
+        copy = remote(at, at, fw_send.at[p, i], fw_recv.at[p, i], sibling)
         copy.start()
         fw_out.append(copy)
-        store(ag.at[core, n], ag_hbm.at[core, n], piece_sem.at[0, i])
-
-    def arrived(i):
+
+    def arrived(p, i):
         n = piece(i)
-        remote(
-            ag.at[other, n], ag.at[other, n], fw_send.at[i], fw_recv.at[i], sibling
-        ).wait_recv()
-        store(ag.at[other, n], ag_hbm.at[other, n], piece_sem.at[1, i])
-
-    to_across(0)
+        at = ag.at[other, n, rows_of(p)]
+        remote(at, at, fw_send.at[p, i], fw_recv.at[p, i], sibling).wait_recv()
+
+    for p, rs in enumerate(parts):
+        x_sent[p * zs + zs - 1].wait_recv()
+        mine = summed(me, rs) + x_in[0, rs].astype(jnp.float32)
+        for o in range(1, zs):
+            z_sent[p * (zs - 1) + o - 1].wait_recv()
+            mine = mine + z_in[o - 1, rs].astype(jnp.float32)
+        if p == 0:
+            ag[core, me, :80] = mine.astype(jnp.bfloat16)
+        else:
+            ag[core, me, 80:144] = mine[:64].astype(jnp.bfloat16)
+            dk[core] = mine[64:]
+        at = ag.at[core, me, rows_of(p)]
+        for o in range(1, zs):
+            copy = remote(at, at, agz_send.at[p, o - 1], agz_recv.at[p, o - 1], along(o)[1])
+            copy.start()
+            agz_out.append(copy)
+        to_across(p, 0)
+        to_sibling(p, 0)
     dk_copy = remote(dk.at[core], dk.at[core], dk_sem.at[0], dk_sem.at[1], sibling)
     dk_copy.start()
-    to_sibling(0)
-    for o in range(1, zs):
-        n = piece(o)
-        remote(
-            ag.at[core, n], ag.at[core, n], agz_send.at[o - 1], agz_recv.at[o - 1], along(o)[1]
-        ).wait_recv()
-        to_across(o)
-        to_sibling(o)
-
-    def from_across(o):
-        n = piece(zs + o)
-        remote(
-            ag.at[core, n], ag.at[core, n], agx_send.at[o], agx_recv.at[o], across
-        ).wait_recv()
-        to_sibling(zs + o)
+    for p in range(2):
+        for o in range(1, zs):
+            at = ag.at[core, piece(o), rows_of(p)]
+            remote(
+                at, at, agz_send.at[p, o - 1], agz_recv.at[p, o - 1], along(o)[1]
+            ).wait_recv()
+            to_across(p, o)
+            to_sibling(p, o)
+
+    def from_across(p, o):
+        at = ag.at[core, piece(zs + o), rows_of(p)]
+        remote(at, at, agx_send.at[p, o], agx_recv.at[p, o], across).wait_recv()
+        to_sibling(p, zs + o)
+
+    for p in range(2):
+        for o in range(zs):
+            from_across(p, o)
 
     remote(dk.at[other], dk.at[other], dk_sem.at[0], dk_sem.at[1], sibling).wait_recv()
     for c in range(2):
         for t in range(3):
             at = (c * 3 + t) * TILE
             gkv[:, at : at + TILE] = dk[c, t * 4 : t * 4 + 4, :]
-    arrived(0)
+    arrived(0, 0)
+    arrived(1, 0)
     for g in range(groups):
         m_own = jnp.concatenate(
             [ag[c, me, t * 48 + g * 16 : t * 48 + g * 16 + 16, :] for c in range(2) for t in range(3)],
@@ -401,11 +426,11 @@
         gkv[:, D + g * 256 : D + g * 256 + 256] = r[:4]
     store(gkv, gkv_hbm.at[0], out_sem.at[3])
 
-    for o in range(zs):
-        from_across(o)
-    for i in range(1, 2 * zs):
-        arrived(i)
-    for copy in kv_out + [swap_pair] + x_sent + z_sent + agz_out + agx_out + fw_out + [dk_copy]:
+    for p in range(2):
+        for i in range(1, 2 * zs):
+            arrived(p, i)
+    store(ag, ag_hbm, out_sem.at[4])
+    for copy in kv_out + swaps + x_sent + z_sent + agz_out + agx_out + fw_out + [dk_copy]:
         copy.wait_send()
     for copy in stores:
         copy.wait()
@@ -456,7 +481,7 @@
     chips = xs * zs
     rows = query_heads.shape[0]
     bf, f32 = jnp.bfloat16, jnp.float32
-    dma = lambda n: pltpu.SemaphoreType.DMA((n,))
+    dma = lambda *n: pltpu.SemaphoreType.DMA(n)
     hbm = pl.BlockSpec(memory_space=pltpu.HBM)
     vmem = pl.BlockSpec(memory_space=pltpu.VMEM)
     limit = 60 * 1024 * 1024
@@ -500,20 +525,19 @@
             dma(5),
             dma(chips - 1),
             dma(chips - 1),
+            dma(2, 2),
+            dma(2, zs),
+            dma(2, zs),
+            dma(2, zs - 1),
+            dma(2, zs - 1),
+            dma(2, zs - 1),
+            dma(2, zs - 1),
+            dma(2, zs),
+            dma(2, zs),
+            dma(2, chips),
+            dma(2, chips),
             dma(2),
-            dma(zs),
-            dma(zs),
-            dma(zs - 1),
-            dma(zs - 1),
-            dma(zs - 1),
-            dma(zs - 1),
-            dma(zs),
-            dma(zs),
-            dma(chips),
-            dma(chips),
-            dma(2),
-            dma(4),
-            pltpu.SemaphoreType.DMA((2, chips)),
+            dma(5),
         ],
         compiler_params=pltpu.CompilerParams(
             collective_id=0, has_side_effects=True, vmem_limit_bytes=limit

time: 34.9 us -> 34.1 us (0.977)
  Pallas kernels: 34 us -> 33.2 us
    pallas_call x1, Pallas kernels: 30.7 us -> 30 us  [fused(): pl.pallas_call(functools.partial(fused_kernel, xs, zs), out_shape=(jax.Sh...]
where the time goes in v3:
time: 34.1 us; the launch traced here: 33.9 us
  Pallas kernels  33.2 us (97%)
  between operations  0.64 us (2%)
    pallas_call x1, Pallas kernels, fused(): pl.pallas_call(functools.partial(fused_kernel, xs, zs), out_shape=(jax.Sh...  30 us
    pallas_call x1, Pallas kernels, fused(): pl.pallas_call(last_kernel, out_shape=(jax.ShapeDtypeStruct((rows, D), bf...  3.26 us

profile of v3, /device:TPU:1, one launch (start us, length us, event | category | flops | bytes accessed | tf_op | source)
XLA Modules:
  0.0 33.9 jit_solution(6994976250172199084)
XLA Ops:
  0.6 30.0 %shard_map.85 = (bf16[2,8,144,128]{3,2,1,0:T(8,128)(2,1)}, f32[1,4,1536]{2,1,0:T(4,128)}, bf16[3,128,256]{2,1,0:T(8,128)(2,1)}, bf16[3,128,256]{2,1,0:T(8,128)(2,1)}, bf16[3,128,512]{2,1,0:T(8,128)(2,1)}) custom-call(s32[1,4]{1,0:T(1,128)} %counts_hbm.1, s32[4]{0:T(128)} %slots_hbm.1, bf16[1,4,1536]{2,1,0:T(4,128)(2,1)} %kv.1, bf16[512,768]{1,0:T(8,128)(2,1)} %q_hbm.1, ...), custom_call_target="tpu_custom_call" | custom-call | flops 1207959552 | bytes 5242880 | tf_op jit(solution)/shard_map/pallas_call | solution.py:492
  30.6 3.3 %shard_map.86 = (bf16[512,768]{1,0:T(8,128)(2,1)}, f32[1,4,1536]{2,1,0:T(4,128)}, f32[768,768]{1,0:T(8,128)}) custom-call(bf16[2,8,144,128]{3,2,1,0:T(8,128)(2,1)} %get-tuple-element.8.ag_hbm, f32[1,4,1536]{2,1,0:T(4,128)} %get-tuple-element.9.gkv_hbm, bf16[3,128,256]{2,1,0:T(8,128)(2,1)} %get-tuple-element.10.kbd_hbm, ...), custom_call_target="tpu_custom_call" | custom-call | flops 603979776 | bytes 5242880 | tf_op jit(solution)/shard_map/pallas_call | solution.py:549

commit v4 on v3

--- a/solution.py
+++ b/solution.py
@@ -179,8 +179,6 @@
         pltpu.make_async_copy(a, b, in_sem.at[i])
         for i, (a, b) in enumerate(((do_hbm, do), (w_hbm, w), (q_hbm, q), (counts_hbm, counts), (slots_hbm, slots)))
     ]
-    for load in loads:
-        load.start()
 
     barrier = pltpu.get_barrier_semaphore()
     for offset in range(1, chips):
@@ -188,6 +186,9 @@
             barrier, inc=1, device_id=chip(offset)[1], device_id_type=pl.DeviceIdType.MESH
         )
     pl.semaphore_signal(barrier, inc=1, device_id=sibling, device_id_type=pl.DeviceIdType.MESH)
+
+    for load in loads:
+        load.start()
 
     own_kv = kv[0].astype(jnp.float32)
     for h in range(HEADS):

time: 34.1 us -> 34.1 us (level)
  no operation moved by 1% of the time
where the time goes in v4:
time: 34.1 us; the launch traced here: 33.8 us
  Pallas kernels  33.2 us (97%)
  between operations  0.64 us (2%)
    pallas_call x1, Pallas kernels, fused(): pl.pallas_call(functools.partial(fused_kernel, xs, zs), out_shape=(jax.Sh...  29.9 us
    pallas_call x1, Pallas kernels, fused(): pl.pallas_call(last_kernel, out_shape=(jax.ShapeDtypeStruct((rows, D), bf...  3.26 us

profile of v4, /device:TPU:1, one launch (start us, length us, event | category | flops | bytes accessed | tf_op | source)
XLA Modules:
  0.0 33.8 jit_solution(15973478087405290698)
XLA Ops:
  0.6 29.9 %shard_map.85 = (bf16[2,8,144,128]{3,2,1,0:T(8,128)(2,1)}, f32[1,4,1536]{2,1,0:T(4,128)}, bf16[3,128,256]{2,1,0:T(8,128)(2,1)}, bf16[3,128,256]{2,1,0:T(8,128)(2,1)}, bf16[3,128,512]{2,1,0:T(8,128)(2,1)}) custom-call(s32[1,4]{1,0:T(1,128)} %counts_hbm.1, s32[4]{0:T(128)} %slots_hbm.1, bf16[1,4,1536]{2,1,0:T(4,128)(2,1)} %kv.1, bf16[512,768]{1,0:T(8,128)(2,1)} %q_hbm.1, ...), custom_call_target="tpu_custom_call" | custom-call | flops 1207959552 | bytes 5242880 | tf_op jit(solution)/shard_map/pallas_call | solution.py:493
  30.6 3.3 %shard_map.86 = (bf16[512,768]{1,0:T(8,128)(2,1)}, f32[1,4,1536]{2,1,0:T(4,128)}, f32[768,768]{1,0:T(8,128)}) custom-call(bf16[2,8,144,128]{3,2,1,0:T(8,128)(2,1)} %get-tuple-element.8.ag_hbm, f32[1,4,1536]{2,1,0:T(4,128)} %get-tuple-element.9.gkv_hbm, bf16[3,128,256]{2,1,0:T(8,128)(2,1)} %get-tuple-element.10.kbd_hbm, ...), custom_call_target="tpu_custom_call" | custom-call | flops 603979776 | bytes 5242880 | tf_op jit(solution)/shard_map/pallas_call | solution.py:550
